TPU v7x, 32 devices: a whole 2x2x4 slice. The times are simulated.
32 devices in a mesh: hid: 8 (over z, x), ffn: 4 (over y, core).
Axes of the slice: x: 2, y: 2, z: 4, core: 2. Of those that a mesh axis runs over, the one named last changes fastest.
Arguments:
- tokens: bfloat16 [256, 8192], P('ffn', 'hid'), may hold values from -128 to 128
- lang_ids: int32 [256], P('ffn'), may hold values from 0 to 15
- gain_table: float32 [16, 8192], P(None, 'hid'), may hold values from 0.1 to 1.9
- gate_weight: bfloat16 [8192, 28672], P('hid', 'ffn'), may hold values from -0.0625 to 0.0625
- up_weight: bfloat16 [8192, 28672], P('hid', 'ffn'), may hold values from -0.0625 to 0.0625
- down_weight: bfloat16 [28672, 8192], P('ffn', 'hid'), may hold values from -0.03125 to 0.03125
Outputs:
- mixed: bfloat16 [256, 8192], P('ffn', 'hid')
All inputs are finite; a program needn't handle non-finite values.
Results may differ from a plain program's by a relative error of at most 0.012.
Values may be sent and summed in bfloat16 or wider, within the bound.
A program may use at most 128 MiB of HBM per device.

v0:
```python
import jax
import jax.numpy as jnp
from jax import lax
from jax.sharding import PartitionSpec as P


def local(tokens, lang_ids, gain_table, gate_weight, up_weight, down_weight):
    hid_count = lax.axis_size("hid")
    unit_count = gate_weight.shape[1]
    feature_total = tokens.shape[1] * hid_count
    one_hot = (
        lang_ids[:, None] == jnp.arange(gain_table.shape[0], dtype=jnp.int32)[None, :]
    ).astype(jnp.float32)
    token_gains = jnp.dot(one_hot, gain_table, precision=lax.Precision.HIGHEST)
    values = tokens.astype(jnp.float32)
    scaled = (values * token_gains).astype(jnp.bfloat16)
    squares = jnp.sum(values * values, axis=1)
    square_pieces = lax.all_gather(squares, "ffn", axis=0, tiled=True)
    all_squares = lax.psum(square_pieces, "hid")
    inverse_rms = lax.rsqrt(all_squares / feature_total + 1e-05)
    both_weights = jnp.concatenate([gate_weight, up_weight], axis=1)
    gathered = lax.all_gather(scaled, "ffn", axis=0, tiled=True)
    partial_sums = jnp.dot(gathered, both_weights, preferred_element_type=jnp.float32)
    summed = lax.psum(partial_sums.astype(jnp.bfloat16), "hid").astype(jnp.float32)
    gate_sum = summed[:, :unit_count] * inverse_rms[:, None]
    up_sum = summed[:, unit_count:] * inverse_rms[:, None]
    hidden = (jax.nn.silu(gate_sum) * up_sum).astype(jnp.bfloat16)
    down_terms = jnp.dot(hidden, down_weight, preferred_element_type=jnp.float32)
    own_rows = lax.psum_scatter(
        down_terms.astype(jnp.bfloat16), "ffn", scatter_dimension=0, tiled=True
    ).astype(jnp.float32)
    return (values + own_rows).astype(jnp.bfloat16)


def solution(mesh):
    return jax.shard_map(
        local,
        mesh=mesh,
        in_specs=(
            P("ffn", "hid"),
            P("ffn"),
            P(None, "hid"),
            P("hid", "ffn"),
            P("hid", "ffn"),
            P("ffn", "hid"),
        ),
        out_specs=P("ffn", "hid"),
        check_vma=False,
    )
```

profile of v0, /device:TPU:1, one launch (start us, length us, event | category | flops | bytes accessed | tf_op | source)
XLA Modules:
  0.0 333.0 jit_solution(15046360407539104117)
XLA Ops:
  6.5 0.0 copy-start
  6.5 0.0 all-reduce.3.cloned.1.call-start
  6.5 0.8 copy-done
  7.4 1.2 fusion.14
  8.6 8.5 %all_gather.6 = bf16[256,1024]{1,0:T(8,128)(2,1)S(1)} all-gather(bf16[64,1024]{1,0:T(8,128)(2,1)S(1)} %fusion.14), channel_id=1, replica_groups=mesh['hid'=8,'ffn'=4] {'ffn'}, dimensions={0}, use_global_device_ids=true | all-gather | bytes 655360 | tf_op jit(solution)/shard_map/all_gather | solution.py:22
  17.1 0.0 copy-start.3
  17.2 0.0 copy-start.2
  17.2 19.5 %fusion.4 = bf16[256,14336]{1,0:T(8,128)(2,1)} fusion(bf16[256,1024]{1,0:T(8,128)(2,1)S(1)} %all_gather.6, bf16[1024,7168]{1,0:T(8,128)(2,1)} %param.10, bf16[1024,7168]{1,0:T(8,128)(2,1)} %param.9), kind=kOutput, calls=%fused_computation.4 | convolution fusion | flops 7578583040 | bytes 37224448 | tf_op jit(solution)/shard_map/dot_general | solution.py:23
  36.6 0.0 all-reduce.3.cloned.1.call-update
  36.7 0.0 reduce-scatter.2.cloned.1.call-start
  36.7 0.0 copy-done.3
  36.7 0.6 dynamic-slice
  38.0 0.0 copy-done.2
  38.0 0.1 fusion.15
  38.1 0.2 dynamic-update-slice
  38.4 5.1 %all-reduce = f32[256]{0:T(256)S(1)} all-reduce(f32[256]{0:T(256)S(1)} %dynamic-update-slice), channel_id=1, replica_groups=mesh['hid'=8,'ffn'=4] {'ffn'}, use_global_device_ids=true, to_apply=%add | all-reduce | flops 256 | bytes 2048
  43.5 18.7 %psum.15 = f32[256]{0:T(256)S(1)} all-reduce(f32[256]{0:T(256)S(1)} %all-reduce), channel_id=1, replica_groups=mesh['hid'=8,'ffn'=4] {'hid'}, use_global_device_ids=true, to_apply=%region_2.0 | all-reduce | flops 256 | bytes 2048 | tf_op jit(solution)/shard_map/psum | solution.py:19
  62.2 216.8 %all-reduce.3.cloned.1.call-done = bf16[256,14336]{1,0:T(8,128)(2,1)} async-done(((bf16[256,14336]{1,0:T(8,128)(2,1)}), bf16[256,14336]{1,0:T(8,128)(2,1)}) %all-reduce.3.cloned.1.call-update) | async-done | bytes 7340048 | tf_op jit(solution)/shard_map/psum | solution.py:24
  279.0 10.0 %convert_element_type.28 = f32[256,14336]{1,0:T(8,128)} convert(bf16[256,14336]{1,0:T(8,128)(2,1)} %all-reduce.3.cloned.1.call-done) | non-fusion elementwise | flops 3670016 | bytes 22020096 | tf_op jit(solution)/shard_map/convert_element_type | solution.py:24
  289.0 0.0 copy-start.1
  289.0 14.6 %fusion.11 = bf16[256,1024]{1,0:T(8,128)(2,1)} fusion(bf16[7168,1024]{1,0:T(8,128)(2,1)} %param.11, f32[256,14336]{1,0:T(8,128)} %convert_element_type.28, f32[256]{0:T(256)S(1)} %add_rsqrt_fusion), kind=kOutput, calls=%fused_computation.10 | convolution fusion | flops 3773038592 | bytes 29885440 | tf_op jit(solution)/shard_map/dot_general | solution.py:28
  303.6 0.0 reduce-scatter.2.cloned.1.call-update
  303.7 20.9 %reduce-scatter.2.cloned.1.call-done = bf16[64,1024]{1,0:T(8,128)(2,1)} async-done(((bf16[256,1024]{1,0:T(8,128)(2,1)}), bf16[64,1024]{1,0:T(8,128)(2,1)}) %reduce-scatter.2.cloned.1.call-update) | async-done | bytes 131088 | tf_op jit(solution)/shard_map/reduce_scatter | solution.py:29
  324.5 1.6 fusion.16
  326.1 0.0 copy-done.1
  (2 shorter events, 0.0 us)
Async XLA Ops:
  6.5 0.8 copy-start
  6.5 272.4 %all-reduce.3.cloned.1.call-start = ((), (), s32[]{:S(2)}) async-start(), calls=%async_computation.1 | async-start | bytes 14680064 | tf_op jit(solution)/shard_map/psum | solution.py:24
  17.1 19.6 %copy-start.3 = (u32[32]{0:T(128)S(1)}, u32[32]{0:T(128)}, u32[]{:S(2)}) copy-start(u32[32]{0:T(128)} %constant.12) | copy-start | bytes 388
  17.2 20.8 %copy-start.2 = (bf16[64,1024]{1,0:T(8,128)(2,1)S(1)}, bf16[64,1024]{1,0:T(8,128)(2,1)}, u32[]{:S(2)}) copy-start(bf16[64,1024]{1,0:T(8,128)(2,1)} %param.6) | copy-start | bytes 393220
  36.7 287.9 %reduce-scatter.2.cloned.1.call-start = ((), (), s32[]{:S(2)}) async-start(), calls=%async_computation.2 | async-start | bytes 655360 | tf_op jit(solution)/shard_map/reduce_scatter | solution.py:29
  289.0 37.1 %copy-start.1 = (f32[16,1024]{1,0:T(8,128)S(1)}, f32[16,1024]{1,0:T(8,128)}, u32[]{:S(2)}) copy-start(f32[16,1024]{1,0:T(8,128)} %param.8) | copy-start | bytes 196612
Sparse Core Ops, SparseCore 0:
  36.8 242.1 all-reduce.2
  303.8 20.7 reduce-scatter.1
where the time goes:
time: 334 us; the launch traced here: 333 us
  waiting for transfers between devices  238 us (71%)
  matrix products  35.3 us (11%)
  blocking collectives  32.3 us (10%)
  between operations  14.1 us (4%)
  other arithmetic  11.8 us (4%)
    psum x1, waiting for transfers between devices, local(): lax.psum(partial_sums.astype(jnp.bfloat16), 'hid').astype(jnp.float32)  217 us
    reduce_scatter x1, waiting for transfers between devices, local(): lax.psum_scatter(down_terms.astype(jnp.bfloat16), 'ffn', scatter_dimensio...  20.9 us
    dot_general x1, matrix products, local(): jnp.dot(gathered, both_weights, preferred_element_type=jnp.float32)  19.5 us
    psum x1, blocking collectives, local(): all_squares = lax.psum(square_pieces, 'hid')  18.7 us
    dot_general x1, matrix products, local(): jnp.dot(hidden, down_weight, preferred_element_type=jnp.float32)  14.6 us
    convert_element_type x1, other arithmetic, local(): lax.psum(partial_sums.astype(jnp.bfloat16), 'hid').astype(jnp.float32)  10 us
    all_gather x1, blocking collectives, local(): gathered = lax.all_gather(scaled, 'ffn', axis=0, tiled=True)  8.54 us
  transfers between devices with their start and end apart: 2, of which 2 were waited for; matrix products, arithmetic and copies ran while one was open for 0% of the time, Pallas kernels for 0%

commit v1 on v0

v1 whole, which is shorter than its diff:
```python
import functools

import jax
import jax.numpy as jnp
from jax import lax
from jax.experimental import pallas as pl
from jax.experimental.pallas import tpu as pltpu
from jax.sharding import PartitionSpec as P

BF16, F32 = jnp.bfloat16, jnp.float32
PIECES = 4
TILE = 256


def gather_then_sum(tokens, lang_ids, gain_table, gate_weight, up_weight, down_weight):
    hid_count = lax.axis_size("hid")
    unit_count = gate_weight.shape[1]
    feature_total = tokens.shape[1] * hid_count
    one_hot = (
        lang_ids[:, None] == jnp.arange(gain_table.shape[0], dtype=jnp.int32)[None, :]
    ).astype(F32)
    token_gains = jnp.dot(one_hot, gain_table, precision=lax.Precision.HIGHEST)
    values = tokens.astype(F32)
    scaled = (values * token_gains).astype(BF16)
    squares = jnp.sum(values * values, axis=1)
    square_pieces = lax.all_gather(squares, "ffn", axis=0, tiled=True)
    all_squares = lax.psum(square_pieces, "hid")
    inverse_rms = lax.rsqrt(all_squares / feature_total + 1e-05)
    both_weights = jnp.concatenate([gate_weight, up_weight], axis=1)
    gathered = lax.all_gather(scaled, "ffn", axis=0, tiled=True)
    partial_sums = jnp.dot(gathered, both_weights, preferred_element_type=F32)
    summed = lax.psum(partial_sums.astype(BF16), "hid").astype(F32)
    gate_sum = summed[:, :unit_count] * inverse_rms[:, None]
    up_sum = summed[:, unit_count:] * inverse_rms[:, None]
    hidden = (jax.nn.silu(gate_sum) * up_sum).astype(BF16)
    down_terms = jnp.dot(hidden, down_weight, preferred_element_type=F32)
    own_rows = lax.psum_scatter(
        down_terms.astype(BF16), "ffn", scatter_dimension=0, tiled=True
    ).astype(F32)
    return (values + own_rows).astype(BF16)


def kernel(
    n, m, tokens_ref, ids_ref, gain_ref, gate_ref, up_ref, down_ref, out_ref,
    xall, wbuf, part, recv, hidden, down, acc, rowinv, squares, inverse, yout, yin,
    xs_sem, xr_sem, w_sem, d_sem, rs_sem, rr_sem, gs_sem, gr_sem,
    qs_sem, qr_sem, is_sem, ir_sem, ys_sem, yr_sem,
):
    h = lax.axis_index("hid")
    f = lax.axis_index("ffn")
    rows, features = tokens_ref.shape
    units = hidden.shape[2]
    half = n // 2
    side = rows * m // 2
    piece = side // PIECES

    odd = lax.rem(h, 2)
    p = (1 - odd) * (h // 2) + odd * (n - (h + 1) // 2)

    def hid_at(q):
        back = q // half
        return (1 - back) * 2 * q + back * (2 * n - 1 - 2 * q)

    right = hid_at(lax.rem(p + 1, n))
    left = hid_at(lax.rem(p + n - 1, n))
    towards = (right, left)

    def weight_copies(s, b):
        offset = n - 1 - s if b == 0 else lax.rem(s + 1, half)
        chunk = lax.rem(p + offset, n)
        slot = 2 * lax.rem(s, 2) + b
        columns = pl.ds(pl.multiple_of(chunk * units, 128), units)
        return [
            pltpu.make_async_copy(
                ref.at[:, columns], wbuf.at[slot, :, pl.ds(i * units, units)], w_sem.at[slot, i]
            )
            for i, ref in enumerate((gate_ref, up_ref))
        ]

    def start_weights(s):
        for b in range(2):
            for copy in weight_copies(s, b):
                copy.start()

    start_weights(0)
    start_weights(1)

    barrier = pltpu.get_barrier_semaphore()
    for i in range(1, n):
        pl.semaphore_signal(barrier, inc=1, device_id={"hid": lax.rem(h + i, n)})
    for i in range(1, m):
        pl.semaphore_signal(barrier, inc=1, device_id={"ffn": lax.rem(f + i, m)})

    values = tokens_ref[...].astype(F32)
    ids = ids_ref[...]
    gains = jnp.zeros((rows, features), F32)
    for lang in range(gain_ref.shape[0]):
        gains = jnp.where(ids == lang, gain_ref[lang : lang + 1, :], gains)
    own_rows = pl.ds(pl.multiple_of(f * rows, rows), rows)
    xall[own_rows, :] = (values * gains).astype(BF16)
    diagonal = lax.broadcasted_iota(jnp.int32, (rows, 128), 0) == lax.broadcasted_iota(
        jnp.int32, (rows, 128), 1
    )
    sums = jnp.sum(values * values, axis=1, keepdims=True)
    in_lanes = jnp.sum(jnp.where(diagonal, sums, 0.0), axis=0, keepdims=True)
    squares[0] = jnp.broadcast_to(in_lanes, (8, 128))

    pl.semaphore_wait(barrier, n - 1 + m - 1)

    def x_copy(i, sender):
        block = xall.at[pl.ds(pl.multiple_of(sender * rows, rows), rows), :]
        return pltpu.make_async_remote_copy(
            src_ref=block, dst_ref=block, send_sem=xs_sem.at[i], recv_sem=xr_sem.at[i],
            device_id={"ffn": lax.rem(f + i, m)},
        )

    def square_copy(i):
        return pltpu.make_async_remote_copy(
            src_ref=squares.at[0], dst_ref=squares.at[i],
            send_sem=qs_sem.at[i], recv_sem=qr_sem.at[i],
            device_id={"hid": lax.rem(h + i, n)},
        )

    def inverse_copy(i, sender):
        return pltpu.make_async_remote_copy(
            src_ref=inverse.at[sender], dst_ref=inverse.at[sender],
            send_sem=is_sem.at[i], recv_sem=ir_sem.at[i],
            device_id={"ffn": lax.rem(f + i, m)},
        )

    for i in range(1, m):
        x_copy(i, f).start()
    for i in range(1, n):
        square_copy(i).start()
    for i in range(1, m):
        x_copy(i, lax.rem(f + m - i, m)).wait_recv()

    def project(s, b):
        offset = n - 1 - s if b == 0 else lax.rem(s + 1, half)
        chunk = lax.rem(p + offset, n)
        slot = 2 * lax.rem(s, 2) + b
        for copy in weight_copies(s, b):
            copy.wait()

        def tile(t, _):
            columns = pl.ds(pl.multiple_of(t * TILE, TILE), TILE)
            part[chunk, :, columns] = jnp.dot(
                xall[...], wbuf[slot, :, columns], preferred_element_type=F32
            ).astype(BF16)
            return 0

        lax.fori_loop(0, 2 * units // TILE, tile, 0)

    def sum_copy(s, d, q):
        chunk = lax.rem(p + n - 1 - s, n) if d == 0 else lax.rem(p + 1 + s, n)
        return chunk, pltpu.make_async_remote_copy(
            src_ref=part.at[chunk, pl.ds(d * side + q * piece, piece), :],
            dst_ref=recv.at[d, s, pl.ds(q * piece, piece), :],
            send_sem=rs_sem.at[d, s, q], recv_sem=rr_sem.at[d, s, q],
            device_id={"hid": towards[d]},
        )

    def pass_sums(s):
        for q in range(PIECES):
            for d in range(2):
                chunk, copy = sum_copy(s, d, q)
                sum_copy(s - 1, d, q)[1].wait_recv()
                here = pl.ds(d * side + q * piece, piece)
                part[chunk, here, :] = (
                    part[chunk, here, :].astype(F32)
                    + recv[d, s - 1, pl.ds(q * piece, piece), :].astype(F32)
                ).astype(BF16)
                copy.start()

    for d in range(2):
        project(0, d)
        for q in range(PIECES):
            sum_copy(0, d, q)[1].start()
    start_weights(2)

    def early(s, _):
        project(s, 0)
        project(s, 1)

        @pl.when(s + 2 < half)
        def _():
            start_weights(s + 2)

        pass_sums(s)
        return 0

    lax.fori_loop(1, half, early, 0)

    def down_copy(c):
        block = pl.ds(c * units, units)
        return pltpu.make_async_copy(down_ref.at[block, :], down.at[block, :], d_sem.at[c])

    for c in range(n):
        down_copy(c).start()

    for i in range(1, n):
        square_copy(i).wait_recv()
    total = squares[0]
    for i in range(1, n):
        total = total + squares[i]
    inverse[f] = lax.rsqrt(total / (features * n) + 1e-05)
    for i in range(1, m):
        inverse_copy(i, f).start()

    def late(s, _):
        pass_sums(s)
        return 0

    lax.fori_loop(half, n - 1, late, 0)

    for i in range(1, m):
        inverse_copy(i, lax.rem(f + m - i, m)).wait_recv()
    for j in range(m):
        column = jnp.sum(
            jnp.where(diagonal, inverse[j, 0:1, :], 0.0), axis=1, keepdims=True
        )
        rowinv[j * rows : (j + 1) * rows, :] = jnp.broadcast_to(column, (rows, 128))

    def hidden_copy(s, d, q):
        chunk = lax.rem(p + n - s, n) if d == 0 else lax.rem(p + s, n)
        block = hidden.at[chunk, pl.ds(d * side + q * piece, piece), :]
        return pltpu.make_async_remote_copy(
            src_ref=block, dst_ref=block,
            send_sem=gs_sem.at[d, s, q], recv_sem=gr_sem.at[d, s, q],
            device_id={"hid": towards[d]},
        )

    def hidden_arrival(s, d, q):
        chunk = lax.rem(p + n - 1 - s, n) if d == 0 else lax.rem(p + 1 + s, n)
        block = hidden.at[chunk, pl.ds(d * side + q * piece, piece), :]
        return pltpu.make_async_remote_copy(
            src_ref=block, dst_ref=block,
            send_sem=gs_sem.at[d, s, q], recv_sem=gr_sem.at[d, s, q],
            device_id={"hid": towards[d]},
        )

    for q in range(PIECES):
        for d in range(2):
            sum_copy(n - 2, d, q)[1].wait_recv()
            here = pl.ds(d * side + q * piece, piece)
            there = pl.ds(q * piece, piece)
            scale = rowinv[d * side + q * piece : d * side + (q + 1) * piece, 0:1]
            gate, up = [
                (
                    part[p, here, i * units : (i + 1) * units].astype(F32)
                    + recv[d, n - 2, there, i * units : (i + 1) * units].astype(F32)
                )
                * scale
                for i in range(2)
            ]
            hidden[p, here, :] = (gate / (1.0 + jnp.exp(-gate)) * up).astype(BF16)
            hidden_copy(0, d, q).start()

    for c in range(n):
        down_copy(c).wait()

    width = acc.shape[1]

    def expand(chunk, first, count, fresh):
        here = pl.ds(first, count)
        weights = pl.ds(pl.multiple_of(chunk * units, 128), units)

        def tile(t, _):
            columns = pl.ds(pl.multiple_of(t * TILE, TILE), TILE)
            term = jnp.dot(
                hidden[chunk, here, :], down[weights, columns], preferred_element_type=F32
            )
            acc[here, columns] = term if fresh else acc[here, columns] + term
            return 0

        lax.fori_loop(0, width // TILE, tile, 0)

    expand(p, 0, 2 * side, True)

    def gather(s, _):
        for q in range(PIECES):
            for d in range(2):
                hidden_arrival(s - 1, d, q).wait_recv()

                @pl.when(s < n - 1)
                def _():
                    hidden_copy(s, d, q).start()

        expand(lax.rem(p + n - s, n), 0, side, False)
        expand(lax.rem(p + s, n), side, side, False)
        return 0

    lax.fori_loop(1, n, gather, 0)

    def y_copy(i):
        return pltpu.make_async_remote_copy(
            src_ref=yout.at[i], dst_ref=yin.at[i],
            send_sem=ys_sem.at[i], recv_sem=yr_sem.at[i],
            device_id={"ffn": lax.rem(f + i, m)},
        )

    for i in range(1, m):
        theirs = pl.ds(pl.multiple_of(lax.rem(f + i, m) * rows, rows), rows)
        yout[i] = acc[theirs, :].astype(BF16)
        y_copy(i).start()
    result = tokens_ref[...].astype(F32) + acc[own_rows, :]
    for i in range(1, m):
        y_copy(i).wait_recv()
        result = result + yin[i].astype(F32)
    out_ref[...] = result.astype(BF16)

    for i in range(1, m):
        y_copy(i).wait_send()
        x_copy(i, f).wait_send()
        inverse_copy(i, f).wait_send()
    for i in range(1, n):
        square_copy(i).wait_send()

    def settle(s, _):
        for q in range(PIECES):
            for d in range(2):
                sum_copy(s, d, q)[1].wait_send()
                hidden_copy(s, d, q).wait_send()
        return 0

    lax.fori_loop(0, n - 1, settle, 0)


def ring(n, m, tokens, lang_ids, gain_table, gate_weight, up_weight, down_weight):
    rows, features = tokens.shape
    units = gate_weight.shape[1] // n
    width = down_weight.shape[1]
    count = rows * m
    side = count // 2
    dma = pltpu.SemaphoreType.DMA
    vmem = pl.BlockSpec(memory_space=pltpu.VMEM)
    hbm = pl.BlockSpec(memory_space=pl.ANY)
    return pl.pallas_call(
        functools.partial(kernel, n, m),
        out_shape=jax.ShapeDtypeStruct((rows, width), BF16),
        in_specs=[vmem, vmem, vmem, hbm, hbm, hbm],
        out_specs=vmem,
        scratch_shapes=[
            pltpu.VMEM((count, features), BF16),
            pltpu.VMEM((4, features, 2 * units), BF16),
            pltpu.VMEM((n, count, 2 * units), BF16),
            pltpu.VMEM((2, n - 1, side, 2 * units), BF16),
            pltpu.VMEM((n, count, units), BF16),
            pltpu.VMEM((n * units, width), BF16),
            pltpu.VMEM((count, width), F32),
            pltpu.VMEM((count, 128), F32),
            pltpu.VMEM((n, 8, 128), F32),
            pltpu.VMEM((m, 8, 128), F32),
            pltpu.VMEM((m, rows, width), BF16),
            pltpu.VMEM((m, rows, width), BF16),
            dma((m,)), dma((m,)),
            dma((4, 2)), dma((n,)),
            dma((2, n - 1, PIECES)), dma((2, n - 1, PIECES)),
            dma((2, n - 1, PIECES)), dma((2, n - 1, PIECES)),
            dma((n,)), dma((n,)),
            dma((m,)), dma((m,)),
            dma((m,)), dma((m,)),
        ],
        compiler_params=pltpu.CompilerParams(
            collective_id=0, has_side_effects=True, vmem_limit_bytes=60 * 2**20
        ),
        cost_estimate=pl.CostEstimate(
            flops=6 * count * features * n * units,
            bytes_accessed=6 * features * n * units,
            transcendentals=count * units,
        ),
    )(tokens, lang_ids[:, None], gain_table, gate_weight, up_weight, down_weight)


def solution(mesh):
    n, m = mesh.shape["hid"], mesh.shape["ffn"]

    def local(tokens, lang_ids, gain_table, gate_weight, up_weight, down_weight):
        rows, features = tokens.shape
        unit_count = gate_weight.shape[1]
        fits = (
            n % 2 == 0 and n >= 6 and m >= 2 and rows <= 128
            and unit_count % (n * 128) == 0
            and rows * m % (2 * PIECES * 16) == 0 and rows % 16 == 0
            and down_weight.shape[1] % TILE == 0 and features % 128 == 0
        )
        form = functools.partial(ring, n, m) if fits else gather_then_sum
        return form(tokens, lang_ids, gain_table, gate_weight, up_weight, down_weight)

    return jax.shard_map(
        local,
        mesh=mesh,
        in_specs=(
            P("ffn", "hid"),
            P("ffn"),
            P(None, "hid"),
            P("hid", "ffn"),
            P("hid", "ffn"),
            P("ffn", "hid"),
        ),
        out_specs=P("ffn", "hid"),
        check_vma=False,
    )
```

time: 334 us -> 137 us (0.41)
  waiting for transfers between devices: 238 us -> 0 us
  Pallas kernels: 0 us -> 134 us
  matrix products: 35.3 us -> 0 us
  blocking collectives: 32.3 us -> 0 us
  between operations: 14.1 us -> 0.01 us
  other arithmetic: 11.8 us -> 0 us
    psum x1 -> x0, waiting for transfers between devices: 217 us -> none  [local(): lax.psum(partial_sums.astype(jnp.bfloat16), 'hid').astype(jnp.float32)]
    pallas_call x0 -> x1, Pallas kernels: none -> 134 us  [ring(): pl.pallas_call(functools.partial(kernel, n, m), out_shape=jax.ShapeDtypeS...]
    dot_general x3 -> x0, matrix products: 35.3 us -> none  [the longest x1 19.5 us: local(): jnp.dot(gathered, both_weights, preferred_element_type=jnp.float32)]
    reduce_scatter x1 -> x0, waiting for transfers between devices: 20.9 us -> none  [local(): lax.psum_scatter(down_terms.astype(jnp.bfloat16), 'ffn', scatter_dimensio...]
    psum x1 -> x0, blocking collectives: 18.7 us -> none  [local(): all_squares = lax.psum(square_pieces, 'hid')]
    convert_element_type x2 -> x0, other arithmetic: 11.6 us -> none  [the longest x1 10 us: local(): lax.psum(partial_sums.astype(jnp.bfloat16), 'hid').astype(jnp.float32)]
    all_gather x1 -> x0, blocking collectives: 8.54 us -> none  [local(): gathered = lax.all_gather(scaled, 'ffn', axis=0, tiled=True)]
    unnamed x1 -> x0, blocking collectives: 5.15 us -> none
  transfers between devices with their start and end apart: 2 -> 0, of which waited for: 2 -> 0; matrix products, arithmetic and copies ran while one was open for 0% -> 0% of each run, Pallas kernels for 0% -> 0%
where the time goes in v1:
time: 137 us
  Pallas kernels  134 us (98%)
  local copies, waits for them, and re-layouts  2.93 us (2%)
    pallas_call x1, Pallas kernels, ring(): pl.pallas_call(functools.partial(kernel, n, m), out_shape=jax.ShapeDtypeS...  134 us

profile of v1, /device:TPU:1, one launch (start us, length us, event | category | flops | bytes accessed | tf_op | source)
XLA Modules:
  0.0 136.9 jit_solution(5931246243277299142)
XLA Ops:
  0.0 1.4 copy.7.ids_ref
  1.4 134.0 %shard_map.64 = bf16[64,1024]{1,0:T(8,128)(2,1)} custom-call(bf16[64,1024]{1,0:T(8,128)(2,1)} %tokens_ref.1, s32[64,1]{1,0:T(8,128)} %copy.7.ids_ref, f32[16,1024]{1,0:T(8,128)} %gain_ref.1, bf16[1024,7168]{1,0:T(8,128)(2,1)} %gate_ref.1, bf16[1024,7168]{1,0:T(8,128)(2,1)} %up_ref.1, bf16[7168,1024]{1,0:T(8,128)(2,1)} %down_ref.1), custom_call_target="tpu_custom_call" | custom-call | flops 11274289152 | bytes 44040192 | tf_op jit(solution)/shard_map/pallas_call | solution.py:338
  135.4 1.6 %copy.9 = bf16[64,1024]{1,0:T(8,128)(2,1)} copy(bf16[64,1024]{1,0:T(8,128)(2,1)} %shard_map.64) | data formatting | bytes 262144

commit v2 on v1

--- a/solution.py
+++ b/solution.py
@@ -107,12 +107,20 @@
 
     pl.semaphore_wait(barrier, n - 1 + m - 1)
 
-    def x_copy(i, sender):
+    mate = f + 1 - 2 * lax.rem(f, 2)
+
+    def x_copy(i, sender, to):
         block = xall.at[pl.ds(pl.multiple_of(sender * rows, rows), rows), :]
         return pltpu.make_async_remote_copy(
             src_ref=block, dst_ref=block, send_sem=xs_sem.at[i], recv_sem=xr_sem.at[i],
-            device_id={"ffn": lax.rem(f + i, m)},
-        )
+            device_id={"ffn": to},
+        )
+
+    def chip_copy(j, sender):
+        return x_copy(j, sender, lax.rem(f + 2 * j, m))
+
+    def onward_copy(j, sender):
+        return x_copy(m // 2 + j, sender, mate)
 
     def square_copy(i):
         return pltpu.make_async_remote_copy(
@@ -128,12 +136,18 @@
             device_id={"ffn": lax.rem(f + i, m)},
         )
 
-    for i in range(1, m):
-        x_copy(i, f).start()
+    for j in range(1, m // 2):
+        chip_copy(j, f).start()
+    x_copy(0, f, mate).start()
     for i in range(1, n):
         square_copy(i).start()
-    for i in range(1, m):
-        x_copy(i, lax.rem(f + m - i, m)).wait_recv()
+    for j in range(1, m // 2):
+        sender = lax.rem(f + m - 2 * j, m)
+        chip_copy(j, sender).wait_recv()
+        onward_copy(j, sender).start()
+    x_copy(0, mate, mate).wait_recv()
+    for j in range(1, m // 2):
+        onward_copy(j, lax.rem(mate + m - 2 * j, m)).wait_recv()
 
     def project(s, b):
         offset = n - 1 - s if b == 0 else lax.rem(s + 1, half)
@@ -160,7 +174,7 @@
             device_id={"hid": towards[d]},
         )
 
-    def pass_sums(s):
+    def pass_sums(s, between=None):
         for q in range(PIECES):
             for d in range(2):
                 chunk, copy = sum_copy(s, d, q)
@@ -171,25 +185,34 @@
                     + recv[d, s - 1, pl.ds(q * piece, piece), :].astype(F32)
                 ).astype(BF16)
                 copy.start()
+            if between is not None:
+                between(q)
 
     for d in range(2):
         project(0, d)
         for q in range(PIECES):
             sum_copy(0, d, q)[1].start()
     start_weights(2)
+    project(1, 0)
+    project(1, 1)
+    start_weights(3)
 
     def early(s, _):
-        project(s, 0)
-        project(s, 1)
-
-        @pl.when(s + 2 < half)
+        def between(q):
+            if q == 0:
+                project(s + 1, 0)
+            if q == PIECES // 2:
+                project(s + 1, 1)
+
+        pass_sums(s, between)
+
+        @pl.when(s + 3 < half)
         def _():
-            start_weights(s + 2)
-
-        pass_sums(s)
+            start_weights(s + 3)
+
         return 0
 
-    lax.fori_loop(1, half, early, 0)
+    lax.fori_loop(1, half - 1, early, 0)
 
     def down_copy(c):
         block = pl.ds(c * units, units)
@@ -206,12 +229,13 @@
     inverse[f] = lax.rsqrt(total / (features * n) + 1e-05)
     for i in range(1, m):
         inverse_copy(i, f).start()
+    acc[...] = jnp.zeros_like(acc)
 
     def late(s, _):
         pass_sums(s)
         return 0
 
-    lax.fori_loop(half, n - 1, late, 0)
+    lax.fori_loop(half - 1, n - 1, late, 0)
 
     for i in range(1, m):
         inverse_copy(i, lax.rem(f + m - i, m)).wait_recv()
@@ -261,58 +285,67 @@
 
     width = acc.shape[1]
 
-    def expand(chunk, first, count, fresh):
+    def expand(chunk, first, count, tiles):
         here = pl.ds(first, count)
         weights = pl.ds(pl.multiple_of(chunk * units, 128), units)
-
-        def tile(t, _):
-            columns = pl.ds(pl.multiple_of(t * TILE, TILE), TILE)
-            term = jnp.dot(
+        for t in tiles:
+            columns = slice(t * TILE, (t + 1) * TILE)
+            acc[here, columns] += jnp.dot(
                 hidden[chunk, here, :], down[weights, columns], preferred_element_type=F32
             )
-            acc[here, columns] = term if fresh else acc[here, columns] + term
-            return 0
-
-        lax.fori_loop(0, width // TILE, tile, 0)
-
-    expand(p, 0, 2 * side, True)
+
+    every = range(width // TILE)
+
+    def behind(s, tiles):
+        expand(lax.rem(p + n - s, n), 0, side, tiles)
+        expand(lax.rem(p + s, n), side, side, tiles)
 
     def gather(s, _):
         for q in range(PIECES):
             for d in range(2):
                 hidden_arrival(s - 1, d, q).wait_recv()
-
-                @pl.when(s < n - 1)
+                hidden_copy(s, d, q).start()
+            behind(s - 1, every[q::PIECES])
+        return 0
+
+    lax.fori_loop(1, n - 1, gather, 0)
+    behind(n - 2, every)
+
+    def y_copy(to, sender):
+        return pltpu.make_async_remote_copy(
+            src_ref=yout.at[to], dst_ref=yin.at[sender],
+            send_sem=ys_sem.at[to], recv_sem=yr_sem.at[sender],
+            device_id={"ffn": to},
+        )
+
+    for q in range(PIECES):
+        for d in range(2):
+            hidden_arrival(n - 2, d, q).wait_recv()
+        if (q + 1) * piece % rows == 0:
+            for d in range(2):
+                j = (d * side + q * piece) // rows
+                chunk = lax.rem(p + 1, n) if d == 0 else lax.rem(p + n - 1, n)
+                expand(chunk, j * rows, rows, every)
+
+                @pl.when(j != f)
                 def _():
-                    hidden_copy(s, d, q).start()
-
-        expand(lax.rem(p + n - s, n), 0, side, False)
-        expand(lax.rem(p + s, n), side, side, False)
-        return 0
-
-    lax.fori_loop(1, n, gather, 0)
-
-    def y_copy(i):
-        return pltpu.make_async_remote_copy(
-            src_ref=yout.at[i], dst_ref=yin.at[i],
-            send_sem=ys_sem.at[i], recv_sem=yr_sem.at[i],
-            device_id={"ffn": lax.rem(f + i, m)},
-        )
-
-    for i in range(1, m):
-        theirs = pl.ds(pl.multiple_of(lax.rem(f + i, m) * rows, rows), rows)
-        yout[i] = acc[theirs, :].astype(BF16)
-        y_copy(i).start()
+                    yout[j] = acc[j * rows : (j + 1) * rows, :].astype(BF16)
+                    y_copy(j, f).start()
+
     result = tokens_ref[...].astype(F32) + acc[own_rows, :]
     for i in range(1, m):
-        y_copy(i).wait_recv()
-        result = result + yin[i].astype(F32)
+        sender = lax.rem(f + i, m)
+        y_copy(sender, sender).wait_recv()
+        result = result + yin[sender].astype(F32)
     out_ref[...] = result.astype(BF16)
 
     for i in range(1, m):
-        y_copy(i).wait_send()
-        x_copy(i, f).wait_send()
+        y_copy(lax.rem(f + i, m), f).wait_send()
         inverse_copy(i, f).wait_send()
+    for j in range(1, m // 2):
+        chip_copy(j, f).wait_send()
+        onward_copy(j, lax.rem(f + m - 2 * j, m)).wait_send()
+    x_copy(0, f, mate).wait_send()
     for i in range(1, n):
         square_copy(i).wait_send()
 
@@ -379,9 +412,10 @@
         rows, features = tokens.shape
         unit_count = gate_weight.shape[1]
         fits = (
-            n % 2 == 0 and n >= 6 and m >= 2 and rows <= 128
+            n % 2 == 0 and n >= 8 and m % 2 == 0 and m >= 4 and rows <= 128
             and unit_count % (n * 128) == 0
             and rows * m % (2 * PIECES * 16) == 0 and rows % 16 == 0
+            and rows % (rows * m // (2 * PIECES)) == 0
             and down_weight.shape[1] % TILE == 0 and features % 128 == 0
         )
         form = functools.partial(ring, n, m) if fits else gather_then_sum

time: 137 us -> 132 us (0.964)
  Pallas kernels: 134 us -> 129 us
    pallas_call x1, Pallas kernels: 134 us -> 129 us  [ring(): pl.pallas_call(functools.partial(kernel, n, m), out_shape=jax.ShapeDtypeS...]
where the time goes in v2:
time: 132 us
  Pallas kernels  129 us (98%)
  local copies, waits for them, and re-layouts  2.93 us (2%)
    pallas_call x1, Pallas kernels, ring(): pl.pallas_call(functools.partial(kernel, n, m), out_shape=jax.ShapeDtypeS...  129 us

profile of v2, /device:TPU:1, one launch (start us, length us, event | category | flops | bytes accessed | tf_op | source)
XLA Modules:
  0.0 132.1 jit_solution(15443446003324971021)
XLA Ops:
  0.0 1.4 %copy.7.ids_ref = s32[64,1]{1,0:T(8,128)} copy(s32[64,1]{0,1:T(1,128)} %bitcast.1) | data formatting | bytes 512 | tf_op jit(solution)/shard_map/broadcast_in_dim | solution.py:405
  1.4 129.2 %shard_map.64 = bf16[64,1024]{1,0:T(8,128)(2,1)} custom-call(bf16[64,1024]{1,0:T(8,128)(2,1)} %tokens_ref.1, s32[64,1]{1,0:T(8,128)} %copy.7.ids_ref, f32[16,1024]{1,0:T(8,128)} %gain_ref.1, bf16[1024,7168]{1,0:T(8,128)(2,1)} %gate_ref.1, bf16[1024,7168]{1,0:T(8,128)(2,1)} %up_ref.1, bf16[7168,1024]{1,0:T(8,128)(2,1)} %down_ref.1), custom_call_target="tpu_custom_call" | custom-call | flops 11274289152 | bytes 44040192 | tf_op jit(solution)/shard_map/pallas_call | solution.py:371
  130.5 1.6 %copy.9 = bf16[64,1024]{1,0:T(8,128)(2,1)} copy(bf16[64,1024]{1,0:T(8,128)(2,1)} %shard_map.64) | data formatting | bytes 262144

commit v3 on v2

--- a/solution.py
+++ b/solution.py
@@ -92,10 +92,14 @@
         pl.semaphore_signal(barrier, inc=1, device_id={"ffn": lax.rem(f + i, m)})
 
     values = tokens_ref[...].astype(F32)
-    ids = ids_ref[...]
+    turned = lax.broadcasted_iota(jnp.int32, (rows, rows), 0) == lax.broadcasted_iota(
+        jnp.int32, (rows, rows), 1
+    )
+    in_row = jnp.broadcast_to(ids_ref[...].reshape(1, rows).astype(F32), (rows, rows))
+    ids = jnp.sum(jnp.where(turned, in_row, 0.0), axis=1, keepdims=True)
     gains = jnp.zeros((rows, features), F32)
     for lang in range(gain_ref.shape[0]):
-        gains = jnp.where(ids == lang, gain_ref[lang : lang + 1, :], gains)
+        gains = jnp.where(ids == float(lang), gain_ref[lang : lang + 1, :], gains)
     own_rows = pl.ds(pl.multiple_of(f * rows, rows), rows)
     xall[own_rows, :] = (values * gains).astype(BF16)
     diagonal = lax.broadcasted_iota(jnp.int32, (rows, 128), 0) == lax.broadcasted_iota(
@@ -149,17 +153,19 @@
     for j in range(1, m // 2):
         onward_copy(j, lax.rem(mate + m - 2 * j, m)).wait_recv()
 
-    def project(s, b):
+    def project(s, b, first=0, count=2 * side, fetched=False):
         offset = n - 1 - s if b == 0 else lax.rem(s + 1, half)
         chunk = lax.rem(p + offset, n)
         slot = 2 * lax.rem(s, 2) + b
-        for copy in weight_copies(s, b):
-            copy.wait()
+        if not fetched:
+            for copy in weight_copies(s, b):
+                copy.wait()
+        here = pl.ds(first, count)
 
         def tile(t, _):
             columns = pl.ds(pl.multiple_of(t * TILE, TILE), TILE)
-            part[chunk, :, columns] = jnp.dot(
-                xall[...], wbuf[slot, :, columns], preferred_element_type=F32
+            part[chunk, here, columns] = jnp.dot(
+                xall[here, :], wbuf[slot, :, columns], preferred_element_type=F32
             ).astype(BF16)
             return 0
 
@@ -189,9 +195,11 @@
                 between(q)
 
     for d in range(2):
-        project(0, d)
+        project(0, d, d * side, side)
         for q in range(PIECES):
             sum_copy(0, d, q)[1].start()
+    for d in range(2):
+        project(0, d, (1 - d) * side, side, True)
     start_weights(2)
     project(1, 0)
     project(1, 1)
@@ -322,14 +330,16 @@
         for d in range(2):
             hidden_arrival(n - 2, d, q).wait_recv()
         if (q + 1) * piece % rows == 0:
-            for d in range(2):
-                j = (d * side + q * piece) // rows
-                chunk = lax.rem(p + 1, n) if d == 0 else lax.rem(p + n - 1, n)
-                expand(chunk, j * rows, rows, every)
+            for away in range(2):
+                d = lax.rem(2 * f // m + 1 + away, 2)
+                j = d * (m // 2) + q * piece // rows
+                chunk = lax.rem(p + 1 + d * (n - 2), n)
+                there = pl.ds(pl.multiple_of(j * rows, rows), rows)
+                expand(chunk, pl.multiple_of(j * rows, rows), rows, every)
 
                 @pl.when(j != f)
                 def _():
-                    yout[j] = acc[j * rows : (j + 1) * rows, :].astype(BF16)
+                    yout[j] = acc[there, :].astype(BF16)
                     y_copy(j, f).start()
 
     result = tokens_ref[...].astype(F32) + acc[own_rows, :]
@@ -402,7 +412,7 @@
             bytes_accessed=6 * features * n * units,
             transcendentals=count * units,
         ),
-    )(tokens, lang_ids[:, None], gain_table, gate_weight, up_weight, down_weight)
+    )(tokens, lang_ids, gain_table, gate_weight, up_weight, down_weight)
 
 
 def solution(mesh):

time: 132 us -> 130 us (0.985)
  local copies, waits for them, and re-layouts: 2.93 us -> 1.57 us
    broadcast_in_dim x1 -> x0, local copies, waits for them, and re-layouts: 1.36 us -> none  [ring(): lang_ids[:, None]]
where the time goes in v3:
time: 130 us
  Pallas kernels  128 us (98%)
  local copies, waits for them, and re-layouts  1.57 us (1%)
    pallas_call x1, Pallas kernels, ring(): pl.pallas_call(functools.partial(kernel, n, m), out_shape=jax.ShapeDtypeS...  128 us

profile of v3, /device:TPU:1, one launch (start us, length us, event | category | flops | bytes accessed | tf_op | source)
XLA Modules:
  0.0 129.8 jit_solution(11819086446125265995)
XLA Ops:
  0.0 128.2 %shard_map.64 = bf16[64,1024]{1,0:T(8,128)(2,1)} custom-call(bf16[64,1024]{1,0:T(8,128)(2,1)} %tokens_ref.1, s32[64]{0:T(128)} %ids_ref.1, f32[16,1024]{1,0:T(8,128)} %gain_ref.1, bf16[1024,7168]{1,0:T(8,128)(2,1)} %gate_ref.1, bf16[1024,7168]{1,0:T(8,128)(2,1)} %up_ref.1, bf16[7168,1024]{1,0:T(8,128)(2,1)} %down_ref.1), custom_call_target="tpu_custom_call" | custom-call | flops 11274289152 | bytes 44040192 | tf_op jit(solution)/shard_map/pallas_call | solution.py:381
  128.2 1.6 %copy.8 = bf16[64,1024]{1,0:T(8,128)(2,1)} copy(bf16[64,1024]{1,0:T(8,128)(2,1)} %shard_map.64) | data formatting | bytes 262144

commit v4 on v3

--- a/solution.py
+++ b/solution.py
@@ -196,12 +196,20 @@
 
     for d in range(2):
         project(0, d, d * side, side)
-        for q in range(PIECES):
+        sum_copy(0, d, 0)[1].start()
+
+    def start_piece(q):
+        for d in range(2):
             sum_copy(0, d, q)[1].start()
-    for d in range(2):
-        project(0, d, (1 - d) * side, side, True)
+
+    project(0, 0, side, side, True)
+    start_piece(1)
+    project(0, 1, 0, side, True)
     start_weights(2)
+    start_piece(2)
     project(1, 0)
+    for q in range(3, PIECES):
+        start_piece(q)
     project(1, 1)
     start_weights(3)
 

time: 130 us -> 130 us (level)
  no operation moved by 1% of the time
where the time goes in v4:
time: 130 us
  Pallas kernels  128 us (98%)
  local copies, waits for them, and re-layouts  1.57 us (1%)
    pallas_call x1, Pallas kernels, ring(): pl.pallas_call(functools.partial(kernel, n, m), out_shape=jax.ShapeDtypeS...  128 us

profile of v4, /device:TPU:1, one launch (start us, length us, event | category | flops | bytes accessed | tf_op | source)
XLA Modules:
  0.0 129.7 jit_solution(7014003869266798623)
XLA Ops:
  0.0 128.2 %shard_map.64 = bf16[64,1024]{1,0:T(8,128)(2,1)} custom-call(bf16[64,1024]{1,0:T(8,128)(2,1)} %tokens_ref.1, s32[64]{0:T(128)} %ids_ref.1, f32[16,1024]{1,0:T(8,128)} %gain_ref.1, bf16[1024,7168]{1,0:T(8,128)(2,1)} %gate_ref.1, bf16[1024,7168]{1,0:T(8,128)(2,1)} %up_ref.1, bf16[7168,1024]{1,0:T(8,128)(2,1)} %down_ref.1), custom_call_target="tpu_custom_call" | custom-call | flops 11274289152 | bytes 44040192 | tf_op jit(solution)/shard_map/pallas_call | solution.py:389
  128.2 1.6 %copy.8 = bf16[64,1024]{1,0:T(8,128)(2,1)} copy(bf16[64,1024]{1,0:T(8,128)(2,1)} %shard_map.64) | data formatting | bytes 262144
